TPU v7x, 32 devices: a whole 2x2x4 slice. The times are simulated.
32 devices in a mesh: dp: 32 (over z, y, x, core).
Axes of the slice: x: 2, y: 2, z: 4, core: 2. Of those that a mesh axis runs over, the one named last changes fastest.
Arguments:
- features: bfloat16 [23360, 40], P('dp'), may hold values from -6 to 6
- ivectors: bfloat16 [128, 100], P('dp'), may hold values from -6 to 6
- frame_mask: int32 [23360], P('dp'), may hold values from 0 to 1, as said below
- labels: int32 [23360], P('dp'), may hold values from 0 to 6015
- confidence: float32 [23360], P('dp'), may hold values from 0.25 to 1
- weights: float32 [32, 101696], P('dp'), as said below
- first_moment: float32 [32, 101696], P('dp'), may hold values from -0.0008544922 to 0.0008544922
- second_moment: float32 [32, 101696], P('dp'), may hold values from 1.532043e-10 to 2.4512687e-09
- biases: float32 [9344], replicated, may hold values from -3 to 3
- bias_first: float32 [9344], replicated, may hold values from -0.0024414062 to 0.0024414062
- bias_second: float32 [9344], replicated, may hold values from 1.3788387e-09 to 2.206142e-08
Outputs:
- new_weights: float32 [32, 101696], P('dp')
- new_first: float32 [32, 101696], P('dp')
- new_second: float32 [32, 101696], P('dp')
- new_biases: float32 [9344], replicated
- new_bias_first: float32 [9344], replicated
- new_bias_second: float32 [9344], replicated
- loss_sum: float32 [], replicated
- loss_weight: float32 [], replicated
- grad_norm: float32 [], replicated
Inputs may be any that keep to these rules, and one draw needn't show every extreme that they name: `frame_mask`: in each span the frames that count form a leading run of at least one frame; some span counts all its frames. Master weights of the five matrices, scaled by their fan-in.
All inputs are finite; a program needn't handle non-finite values.
Results may differ from a plain program's by a relative error of at most 0.0066.
Values may be sent and summed in bfloat16 or wider, within the bound.
No kernel may reach another device: no remote copies, remote signals or barrier semaphores. Data moves between devices by JAX's collectives and lax.ppermute only.
A program may use at most 256 MiB of HBM per device.

v0:
```python
import jax
import jax.numpy as jnp
from jax import lax
from jax.sharding import PartitionSpec as P

FEAT = 40
IVEC = 100
HID = 1536
BOT = 160
PRE = 256
SEN = 6016
L1 = 140
L2 = 150
L3 = 300
C1 = 2
C2 = 1
C3 = 1
STEP = 10


bypass_scale = 0.66
norm_eps = 0.001
learn_rate = 0.05
beta_one = 0.9
beta_two = 0.999
adam_eps = 1e-08
decay_rate = 0.01
clip_norm = 1.0


def earlier(v):
    return jnp.pad(v, ((0, 0), (1, 0), (0, 0)))[:, :-1]


def later(v):
    return jnp.pad(v, ((0, 0), (0, 1), (0, 0)))[:, 1:]


def unpack(flat):
    shapes = [(3 * FEAT + IVEC, HID), (2 * HID, BOT), (2 * BOT, HID), (HID, PRE), (PRE, SEN)]
    result = []
    start = 0
    for rows, cols in shapes:
        result.append(flat[start : start + rows * cols].reshape(rows, cols))
        start = start + rows * cols
    return result


def split_bias(bias):
    return (bias[:HID], bias[HID : 2 * HID], bias[2 * HID : 2 * HID + PRE], bias[2 * HID + PRE :])


def product(left, right):
    return jnp.dot(left, right, preferred_element_type=jnp.float32)


def product_left(left, right):
    return lax.dot_general(
        left, right, (((0,), (0,)), ((), ())), preferred_element_type=jnp.float32
    )


def product_right(left, right):
    return lax.dot_general(
        left, right, (((1,), (1,)), ((), ())), preferred_element_type=jnp.float32
    )


def gelu_back(value, grad):
    return jax.vjp(jax.nn.gelu, value)[1](grad)[0]


def normalize(hidden, mask):
    wide = mask[:, None]
    sums, squares, count = lax.psum(
        (jnp.sum(wide * hidden, axis=0), jnp.sum(wide * hidden * hidden, axis=0), jnp.sum(mask)),
        "dp",
    )
    mean = sums / count
    var = squares / count - mean * mean
    scale = lax.rsqrt(var + norm_eps)
    return ((hidden - mean) * scale, scale, count)


def normalize_back(grad, normed, scale, count, mask):
    along, cross = lax.psum((jnp.sum(grad, axis=0), jnp.sum(grad * normed, axis=0)), "dp")
    return scale * (grad - mask[:, None] / count * (along + cross * normed))


def micro_step(mats, parts, feats, ivecs, mask, labels, confidence, fetch):
    w_in, w_first, w_second, w_pre, w_out = mats
    b_in, b_second, b_pre, b_out = parts
    spans, length = (feats.shape[0], feats.shape[1])
    rows = spans * length
    ivec_wide = jnp.broadcast_to(ivecs[:, None, :], (spans, length, IVEC))
    spliced = jnp.concatenate([earlier(feats), feats, later(feats), ivec_wide], axis=-1).reshape(
        rows, 3 * FEAT + IVEC
    )
    act_in = product(spliced, w_in) + b_in
    norm_in, scale_in, count = normalize(jax.nn.gelu(act_in), mask)
    rounded = norm_in.astype(jnp.bfloat16).reshape(spans, length, HID)
    joined = jnp.concatenate([earlier(rounded), rounded], axis=-1).reshape(rows, 2 * HID)
    factor = product(joined, w_first).astype(jnp.bfloat16).reshape(spans, length, BOT)
    paired = jnp.concatenate([factor, later(factor)], axis=-1).reshape(rows, 2 * BOT)
    act_mid = product(paired, w_second) + b_second
    norm_mid, scale_mid, unused = normalize(jax.nn.gelu(act_mid), mask)
    summed = (norm_mid + bypass_scale * norm_in).astype(jnp.bfloat16)
    pre = (product(summed, w_pre) + b_pre).astype(jnp.bfloat16)
    logits = product(pre, w_out) + b_out
    top = jnp.max(logits, axis=-1, keepdims=True)
    expo = jnp.exp(logits - top)
    total = jnp.sum(expo, axis=-1, keepdims=True)
    lse = jnp.log(total[:, 0]) + top[:, 0]
    onehot = labels[:, None] == lax.broadcasted_iota(jnp.int32, (1, SEN), 1)
    picked = jnp.sum(jnp.where(onehot, logits, 0.0), axis=-1)
    weight = confidence * mask
    loss = jnp.sum(weight * (lse - picked))
    d_logits = (weight[:, None] * (expo / total - onehot.astype(jnp.float32))).astype(jnp.bfloat16)
    w_in, w_first, w_second, w_pre, w_out = fetch()
    g_out = product_left(pre, d_logits)
    gb_out = jnp.sum(d_logits.astype(jnp.float32), axis=0)
    d_pre = product_right(d_logits, w_out).astype(jnp.bfloat16)
    g_pre = product_left(summed, d_pre)
    gb_pre = jnp.sum(d_pre.astype(jnp.float32), axis=0)
    d_sum = product_right(d_pre, w_pre)
    d_mid = normalize_back(d_sum, norm_mid, scale_mid, count, mask)
    d_act_mid = gelu_back(act_mid, d_mid).astype(jnp.bfloat16)
    g_second = product_left(paired, d_act_mid)
    gb_second = jnp.sum(d_act_mid.astype(jnp.float32), axis=0)
    d_paired = product_right(d_act_mid, w_second).reshape(spans, length, 2 * BOT)
    d_factor = (
        (d_paired[..., :BOT] + earlier(d_paired[..., BOT:])).astype(jnp.bfloat16).reshape(rows, BOT)
    )
    g_first = product_left(joined, d_factor)
    d_joined = product_right(d_factor, w_first).reshape(spans, length, 2 * HID)
    d_norm_in = bypass_scale * d_sum + (d_joined[..., HID:] + later(d_joined[..., :HID])).reshape(
        rows, HID
    )
    d_in = normalize_back(d_norm_in, norm_in, scale_in, count, mask)
    d_act_in = gelu_back(act_in, d_in).astype(jnp.bfloat16)
    g_in = product_left(spliced, d_act_in)
    gb_in = jnp.sum(d_act_in.astype(jnp.float32), axis=0)
    grads = jnp.concatenate(
        [
            g_in.reshape(-1),
            g_first.reshape(-1),
            g_second.reshape(-1),
            g_pre.reshape(-1),
            g_out.reshape(-1),
        ]
    )
    bias_grad = jnp.concatenate([gb_in, gb_second, gb_pre, gb_out])
    return (grads, bias_grad, loss)


def adam(value, grad, first, second, decay):
    first = beta_one * first + (1.0 - beta_one) * grad
    second = beta_two * second + (1.0 - beta_two) * grad * grad
    first_hat = first / (1.0 - beta_one**STEP)
    second_hat = second / (1.0 - beta_two**STEP)
    value = value - learn_rate * (first_hat / (jnp.sqrt(second_hat) + adam_eps) + decay * value)
    return (value, first, second)


def on_device(
    features,
    ivectors,
    frame_mask,
    labels,
    confidence,
    weights,
    first_moment,
    second_moment,
    biases,
    bias_first,
    bias_second,
):
    devices = lax.axis_size("dp")
    shard = weights.astype(jnp.bfloat16)
    mats = unpack(lax.all_gather(shard, "dp", axis=0, tiled=True).reshape(-1))
    parts = split_bias(biases)

    def fetch():
        return unpack(lax.all_gather(shard, "dp", axis=0, tiled=True).reshape(-1))

    mask_all = frame_mask.astype(jnp.float32)
    shard_grad = jnp.zeros_like(weights)
    bias_total = jnp.zeros_like(biases)
    loss_total = jnp.float32(0.0)
    frame = 0
    span = 0
    for spans, length in ((C1, L1), (C2, L2), (C3, L3)):
        rows = spans * length
        feats = features[frame : frame + rows].reshape(spans, length, FEAT)
        grads, bias_grad, loss = micro_step(
            mats,
            parts,
            feats,
            ivectors[span : span + spans],
            mask_all[frame : frame + rows],
            labels[frame : frame + rows],
            confidence[frame : frame + rows],
            fetch,
        )
        shard_grad = shard_grad + lax.psum_scatter(
            grads.reshape(devices, -1), "dp", scatter_dimension=0, tiled=True
        )
        bias_total = bias_total + bias_grad
        loss_total = loss_total + loss
        frame = frame + rows
        span = span + spans
    squares, bias_sum, loss_sum, loss_weight = lax.psum(
        (jnp.sum(shard_grad * shard_grad), bias_total, loss_total, jnp.sum(confidence * mask_all)),
        "dp",
    )
    grad_norm = jnp.sqrt(squares + jnp.sum(bias_sum * bias_sum))
    scale = jnp.minimum(jnp.float32(1.0), clip_norm / grad_norm)
    new_w, new_m, new_v = adam(weights, shard_grad * scale, first_moment, second_moment, decay_rate)
    new_b, new_bm, new_bv = adam(biases, bias_sum * scale, bias_first, bias_second, 0.0)
    return (new_w, new_m, new_v, new_b, new_bm, new_bv, loss_sum, loss_weight, grad_norm)


def solution(mesh):
    return jax.shard_map(
        on_device,
        mesh=mesh,
        in_specs=(
            P("dp", None),
            P("dp", None),
            P("dp"),
            P("dp"),
            P("dp"),
            P("dp", None),
            P("dp", None),
            P("dp", None),
            P(),
            P(),
            P(),
        ),
        out_specs=(P("dp", None), P("dp", None), P("dp", None), P(), P(), P(), P(), P(), P()),
        check_vma=False,
    )
```

profile of v0, /device:TPU:0, one launch (start us, length us, event | category | flops | bytes accessed | tf_op | source)
XLA Modules:
  0.0 1019.3 jit_solution(2487853790806175785)
XLA Ops:
  32.0 80.4 %all-gather.3.cloned.1.call-done = bf16[32,1,101696]{2,1,0:T(2,128)(2,1)} async-done(((bf16[1,1,101696]{2,1,0:T(2,128)(2,1)}), bf16[32,1,101696]{2,1,0:T(2,128)(2,1)}) %all-gather.3.cloned.1.call-update) | async-done | bytes 6508560 | tf_op jit(solution)/shard_map/all_gather | solution.py:180
  112.4 135.9 %reduce = bf16[32,101696]{1,0:T(8,128)(2,1)} reduce(bf16[32,1,101696]{2,1,0:T(2,128)(2,1)} %all-gather.3.cloned.1.call-done, bf16[]{:T(256)} %constant.119), dimensions={1}, to_apply=%all-gather.reduce_sub_computation | reduce | bytes 13017090 | tf_op jit(solution)/shard_map/all_gather | solution.py:180
  248.4 11.5 %reshape.254 = bf16[3254272]{0:T(1024)(128)(2,1)} reshape(bf16[32,101696]{1,0:T(8,128)(2,1)} %reduce) | data formatting | bytes 13017088 | tf_op jit(solution)/shard_map/reshape | solution.py:180
  262.5 10.6 %slice.190 = bf16[12712,256]{1,0:T(8,128)(2,1)} reshape(bf16[3254272]{0:T(1024)(128)(2,1)} %reshape.254) | data formatting | bytes 13017088 | tf_op jit(solution)/shard_map/slice | solution.py:44
  291.4 40.4 %all-reduce.23 = (f32[1536]{0:T(1024)S(1)}, f32[]{:T(128)}, f32[1536]{0:T(1024)S(1)}, f32[1536]{0:T(1024)S(1)}, f32[]{:T(128)}, /*index=5*/f32[1536]{0:T(1024)S(1)}, f32[1536]{0:T(1024)}, f32[]{:T(128)}, f32[1536]{0:T(1024)}) all-reduce(f32[1536]{0:T(1024)S(1)} %copy-done.159, ...), channel_id=1, replica_groups=mesh['dp'=32] {'dp'}, use_global_device_ids=true, to_apply=%region_47.48 | all-reduce | flops 9219 | bytes 73752 | tf_op jit(solution)/shard_map/psum | solution.py:75
  354.4 5.4 reshape.260
  359.9 41.8 %all-reduce.22 = (f32[1536]{0:T(1024)S(1)}, f32[1536]{0:T(1024)S(1)}, f32[1536]{0:T(1024)S(1)}, f32[1536]{0:T(1024)S(1)}, f32[1536]{0:T(1024)S(1)}, /*index=5*/f32[1536]{0:T(1024)S(1)}) all-reduce(f32[1536]{0:T(1024)S(1)} %copy-done.163, f32[1536]{0:T(1024)S(1)} %copy-done.162, ...), channel_id=1, replica_groups=mesh['dp'=32] {'dp'}, use_global_device_ids=true, to_apply=%region_51.52 | all-reduce | flops 9216 | bytes 73728 | tf_op jit(solution)/shard_map/psum | solution.py:75
  448.6 40.5 %all-reduce.21 = (f32[1536]{0:T(1024)S(1)}, f32[1536]{0:T(1024)S(1)}, f32[1536]{0:T(1024)}, f32[1536]{0:T(1024)}, f32[1536]{0:T(1024)S(1)}, /*index=5*/f32[1536]{0:T(1024)S(1)}) all-reduce(f32[1536]{0:T(1024)S(1)} %get-tuple-element.24, f32[1536]{0:T(1024)S(1)} %get-tuple-element.23, ...), channel_id=1, replica_groups=mesh['dp'=32] {'dp'}, use_global_device_ids=true, to_apply=%region_57.58 | all-reduce | flops 9216 | bytes 73728 | tf_op jit(solution)/shard_map/psum | solution.py:86
  489.1 4.3 convert_reduce_fusion.3
  503.9 4.3 fusion.144
  521.9 4.4 fusion.142
  555.9 41.6 %all-reduce.20 = (f32[1536]{0:T(1024)S(1)}, f32[1536]{0:T(1024)S(1)}, f32[1536]{0:T(1024)}, f32[1536]{0:T(1024)}, f32[1536]{0:T(1024)}, /*index=5*/f32[1536]{0:T(1024)}) all-reduce(f32[1536]{0:T(1024)S(1)} %get-tuple-element.22, f32[1536]{0:T(1024)S(1)} %get-tuple-element.21, ...), channel_id=1, replica_groups=mesh['dp'=32] {'dp'}, use_global_device_ids=true, to_apply=%region_61.62 | all-reduce | flops 9216 | bytes 73728 | tf_op jit(solution)/shard_map/psum | solution.py:86
  603.2 4.9 reshape.295
  612.3 7.4 reshape.298
  625.1 4.9 reshape.263
  634.1 7.1 reshape.266
  656.4 7.2 reshape.282
  669.1 5.8 constant_dynamic-update-slice_fusion.2
  693.6 4.1 copy-done.11
  697.8 10.3 %add_add_fusion = f32[3254272]{0:T(1024)} fusion(f32[3254272]{0:T(1024)S(1)} %bitcast.162, f32[3254272]{0:T(1024)S(1)} %copy-done.11, f32[3254272]{0:T(1024)} %constant_dynamic-update-slice_fusion.1), kind=kLoop, calls=%fused_computation | loop fusion | flops 6508544 | bytes 52068352 | tf_op jit(solution)/shard_map/add | solution.py:205
  708.1 15.5 %reshape.301 = f32[32,101696]{1,0:T(8,128)} reshape(f32[3254272]{0:T(1024)} %add_add_fusion) | data formatting | bytes 26034176 | tf_op jit(solution)/shard_map/add | solution.py:205
  726.9 231.8 %all-reduce.26.cloned.1.call-done = f32[32,101696]{1,0:T(8,128)} async-done(((f32[32,101696]{1,0:T(8,128)}), f32[32,101696]{1,0:T(8,128)}) %all-reduce.26.cloned.1.call-update) | async-done | bytes 13017104
  962.0 41.0 %all-reduce.19 = (f32[]{:T(128)}, f32[9344]{0:T(1024)S(1)}, f32[]{:T(128)}, f32[]{:T(128)}) all-reduce(f32[]{:T(128)} %multiply_reduce_fusion.12, f32[9344]{0:T(1024)S(1)} %fusion.100, f32[]{:T(128)S(6)} %add.504, f32[]{:T(128)} %multiply_reduce_fusion.14), channel_id=1, replica_groups=mesh['dp'=32] {'dp'}, use_global_device_ids=true, to_apply=%region_64.65 | all-reduce | flops 9347 | bytes 74776 | tf_op jit(solution)/shard_map/psum | solution.py:212
  1005.7 5.1 multiply_subtract_fusion
  (554 shorter events, 232.2 us)
Async XLA Ops:
  7.2 12.9 %slice-start.13 = ((bf16[4,100]{1,0:T(4,128)(2,1)}), bf16[2,100]{1,0:T(2,128)(2,1)S(1)}, s32[]{:S(2)}) async-start(bf16[4,100]{1,0:T(4,128)(2,1)} %param.12), calls=%async_computation.15 | async-start | bytes 1024 | tf_op jit(solution)/shard_map/slice | solution.py:199
  7.2 18.5 %copy-start.174 = (bf16[4,100]{1,0:T(4,128)(2,1)S(1)}, bf16[4,100]{1,0:T(4,128)(2,1)}, u32[]{:S(2)}) copy-start(bf16[4,100]{1,0:T(4,128)(2,1)} %param.12) | copy-start | bytes 2404
  7.2 105.2 %all-gather.3.cloned.1.call-start = ((), (), s32[]{:S(2)}) async-start(), calls=%async_computation | async-start | bytes 13432320 | tf_op jit(solution)/shard_map/all_gather | solution.py:180
  9.3 949.4 %all-reduce.26.cloned.1.call-start = ((), (), s32[]{:S(2)}) async-start(), calls=%async_computation.1 | async-start | bytes 26050560
  18.5 265.3 %copy-start.89 = (bf16[1,300,40]{2,1,0:T(8,128)(2,1)}, bf16[1,300,40]{2,1,0:T(8,128)(2,1)S(1)}, u32[]{:S(2)}) copy-start(bf16[1,300,40]{2,1,0:T(8,128)(2,1)S(1)} %copy.71) | copy-start | bytes 72004
  283.8 67.1 %copy-start.5 = (bf16[3072,160]{1,0:T(8,128)(2,1)}, bf16[3072,160]{1,0:T(8,128)(2,1)S(1)}, u32[]{:S(2)}) copy-start(bf16[3072,160]{1,0:T(8,128)(2,1)S(1)} %reshape.257) | copy-start | bytes 2949124
  287.4 45.1 %copy-start = (f32[300,1536]{1,0:T(8,128)}, f32[300,1536]{1,0:T(8,128)S(1)}, u32[]{:S(2)}) copy-start(f32[300,1536]{1,0:T(8,128)S(1)} %get-tuple-element.135) | copy-start | bytes 5529604
  332.4 70.0 %copy-start.103 = (f32[1536]{0:T(1024)}, f32[1536]{0:T(1024)S(1)}, u32[]{:S(2)}) copy-start(f32[1536]{0:T(1024)S(1)} %get-tuple-element.123) | copy-start | bytes 18436
  336.5 87.0 %copy-start.111 = (f32[1536]{0:T(1024)}, f32[1536]{0:T(1024)S(1)}, u32[]{:S(2)}) copy-start(f32[1536]{0:T(1024)S(1)} %get-tuple-element.156) | copy-start | bytes 18436
  336.5 87.0 %copy-start.114 = (f32[1536]{0:T(1024)}, f32[1536]{0:T(1024)S(1)}, u32[]{:S(2)}) copy-start(f32[1536]{0:T(1024)S(1)} %get-tuple-element.157) | copy-start | bytes 18436
  336.5 102.2 %copy-start.105 = (f32[1536]{0:T(1024)}, f32[1536]{0:T(1024)S(1)}, u32[]{:S(2)}) copy-start(f32[1536]{0:T(1024)S(1)} %get-tuple-element.118) | copy-start | bytes 18436
  336.5 102.2 %copy-start.108 = (f32[1536]{0:T(1024)}, f32[1536]{0:T(1024)S(1)}, u32[]{:S(2)}) copy-start(f32[1536]{0:T(1024)S(1)} %get-tuple-element.119) | copy-start | bytes 18436
  423.4 12.5 %copy-start.131 = (f32[1536]{0:T(1024)}, f32[1536]{0:T(1024)S(1)}, u32[]{:S(2)}) copy-start(f32[1536]{0:T(1024)S(1)} %get-tuple-element.115) | copy-start | bytes 18436
  443.1 83.2 %copy-start.151 = (f32[150]{0:T(256)}, f32[150]{0:T(256)S(1)}, u32[]{:S(2)}) copy-start(f32[150]{0:T(256)S(1)} %get-tuple-element.124) | copy-start | bytes 1804
  447.1 42.1 %copy-start.31 = (f32[300,1536]{1,0:T(8,128)S(1)}, f32[300,1536]{1,0:T(8,128)}, u32[]{:S(2)}) copy-start(f32[300,1536]{1,0:T(8,128)} %get-tuple-element.138) | copy-start | bytes 5529604
  447.1 42.1 %copy-start.145 = (f32[300]{0:T(512)S(1)}, f32[300]{0:T(512)}, u32[]{:S(2)}) copy-start(f32[300]{0:T(512)} %get-tuple-element.126) | copy-start | bytes 3604
  667.9 12.6 %slice-start.1 = ((s8[6160384]{0:T(1024)(128)(4,1)}), s8[4194304]{0:T(1024)(128)(4,1)S(1)}, s32[]{:S(2)}) async-start(s8[6160384]{0:T(1024)(128)(4,1)} %bitcast.157), calls=%async_computation.3 | async-start | bytes 8388608
  680.6 12.5 %slice-start.5 = ((s8[13017088]{0:T(1024)(128)(4,1)}), s8[4194304]{0:T(1024)(128)(4,1)S(1)}, s32[]{:S(2)}) async-start(s8[13017088]{0:T(1024)(128)(4,1)} %bitcast.161), calls=%async_computation.7 | async-start | bytes 8388608
  723.7 281.3 %copy-start.117 = (f32[9344]{0:T(1024)S(1)}, f32[9344]{0:T(1024)}, u32[]{:S(2)}) copy-start(f32[9344]{0:T(1024)} %param.19) | copy-start | bytes 112132
  723.7 281.3 %copy-start.137 = (f32[9344]{0:T(1024)S(1)}, f32[9344]{0:T(1024)}, u32[]{:S(2)}) copy-start(f32[9344]{0:T(1024)} %param.20) | copy-start | bytes 112132
  723.7 281.3 %copy-start.138 = (f32[9344]{0:T(1024)S(1)}, f32[9344]{0:T(1024)}, u32[]{:S(2)}) copy-start(f32[9344]{0:T(1024)} %param.21) | copy-start | bytes 112132
  723.8 281.9 %copy-start.66 = (f32[1,101696]{1,0:T(1,128)S(1)}, f32[1,101696]{1,0:T(1,128)}, u32[]{:S(2)}) copy-start(f32[1,101696]{1,0:T(1,128)} %param.16) | copy-start | bytes 1220356
  723.8 281.9 %copy-start.83 = (f32[1,101696]{1,0:T(1,128)S(1)}, f32[1,101696]{1,0:T(1,128)}, u32[]{:S(2)}) copy-start(f32[1,101696]{1,0:T(1,128)} %param.17) | copy-start | bytes 1220356
  723.8 281.9 %copy-start.84 = (f32[1,101696]{1,0:T(1,128)S(1)}, f32[1,101696]{1,0:T(1,128)}, u32[]{:S(2)}) copy-start(f32[1,101696]{1,0:T(1,128)} %param.18) | copy-start | bytes 1220356
  (172 other events, 619.7 us)
Sparse Core Ops, SparseCore 0:
  11.5 100.8 all-gather.2
  723.9 234.6 all-reduce.25
where the time goes:
time: 1030 us; the launch traced here: 1020 us
  waiting for transfers between devices  312 us (30%)
  other arithmetic  221 us (21%)
  blocking collectives  205 us (20%)
  local copies, waits for them, and re-layouts  182 us (18%)
  matrix products  78 us (8%)
  between operations  20.8 us (2%)
    unnamed x3, waiting for transfers between devices  232 us
    all_gather x1, other arithmetic, on_device(): mats = unpack(lax.all_gather(shard, 'dp', axis=0, tiled=True).reshape(-1))  136 us
    psum x2, blocking collectives, normalize(): lax.psum((jnp.sum(wide * hidden, axis=0), jnp.sum(wide * hidden * hidden,...  82.2 us
    psum x2, blocking collectives, normalize_back(): lax.psum((jnp.sum(grad, axis=0), jnp.sum(grad * normed, axis=0)), 'dp')  82.1 us
    all_gather x1, waiting for transfers between devices, on_device(): mats = unpack(lax.all_gather(shard, 'dp', axis=0, tiled=True).reshape(-1))  80.4 us
    unnamed x396, local copies, waits for them, and re-layouts  43.9 us
    psum x1, blocking collectives, on_device(): lax.psum((jnp.sum(shard_grad * shard_grad), bias_total, loss_total, jnp.s...  41 us
    dot_general x15, matrix products, product_left(): lax.dot_general(left, right, (((0,), (0,)), ((), ())), preferred_element_...  34 us
  transfers between devices with their start and end apart: 2, of which 2 were waited for; matrix products, arithmetic and copies ran while one was open for 2% of the time, Pallas kernels for 0%

commit v1 on v0

v1 whole, which is shorter than its diff:
```python
import math

import jax
import jax.numpy as jnp
from jax import lax
from jax.experimental import pallas as pl
from jax.experimental.pallas import tpu as pltpu
from jax.sharding import PartitionSpec as P

FEAT = 40
IVEC = 100
HID = 1536
BOT = 160
PRE = 256
SEN = 6016
SPAN = (140, 140, 150, 300)
START = (0, 144, 288, 448)
ROWS = 768
SEGS = ((0, 288), (288, 448), (448, 768))
SENP = 6144
STEP = 10
NBIAS = 9344

bypass_scale = 0.66
norm_eps = 0.001
learn_rate = 0.05
beta_one = 0.9
beta_two = 0.999
adam_eps = 1e-08
decay_rate = 0.01
clip_norm = 1.0

F32 = jnp.float32
BF = jnp.bfloat16
VM = pl.BlockSpec(memory_space=pltpu.VMEM)
ANY = pl.BlockSpec(memory_space=pl.ANY)
SM = pl.BlockSpec(memory_space=pltpu.SMEM)

CHIP = 1589
BLK = 800
LAYERS = (0, 1, 3, 2)
OFF = (0, 2640, 6480, 10320, 13392)
ROWS_ALL = 16 * CHIP
TILE = 256
NT = HID // TILE
WIDE = 512
NW = SENP // WIDE
GELU_C = math.sqrt(2.0 / math.pi)


def shape(dims, kind=F32):
    return jax.ShapeDtypeStruct(dims, kind)


def params(mb=60):
    return pltpu.CompilerParams(vmem_limit_bytes=mb * 2**20)


def dot(a, b):
    return jnp.dot(a, b, preferred_element_type=F32)


def dot_nt(a, b):
    return lax.dot_general(a, b, (((1,), (1,)), ((), ())), preferred_element_type=F32)


def at(j, size):
    return pl.ds(pl.multiple_of(j * size, size), size)


def unpack_kernel(me, *refs):
    arrs = refs[:8]
    win, w1a, w1b, w2a, w2b, wp, wo = refs[8:15]
    stage, flat, tall, tall2, sem = refs[15:]
    copies = []
    for i in range(8):
        for j in range(4):
            z = lax.rem(me[0] + (4 - LAYERS[i % 4]), 4)
            y = me[1] ^ (j >> 1)
            x = me[2] ^ (j & 1)
            c = me[3] ^ (i // 4)
            d = ((z * 2 + y) * 2 + x) * 2 + c
            copy = pltpu.make_async_copy(arrs[i].at[j], stage.at[d], sem.at[i * 4 + j])
            copy.start()
            copies.append(copy)
    for copy in copies:
        copy.wait()
    for b in range(32):
        base = CHIP * (b // 2) + 794 * (b % 2)
        v = stage[b].astype(F32)
        if b % 2 == 0:
            flat[base : base + 795, :] = v[:795]
        else:
            flat[base : base + 1, :] = flat[base : base + 1, :] + v[0:1]
            flat[base + 1 : base + 795, :] = v[1:795]
    for j in range(12):
        v = flat[pl.ds(j, 224, stride=12), :]
        v = jnp.where(lax.broadcasted_iota(jnp.int32, (224, 128), 0) < 220, v, 0.0)
        win[0:224, 128 * j : 128 * j + 128] = v.astype(BF)
    win[224:256, :] = jnp.zeros((32, HID), BF)
    for j in range(12):
        v = flat[pl.ds(OFF[2] + j, 320, stride=12), :].astype(BF)
        w2a[0:160, 128 * j : 128 * j + 128] = v[:160]
        w2b[0:160, 128 * j : 128 * j + 128] = v[160:]
    w2a[160:256, :] = jnp.zeros((96, HID), BF)
    w2b[160:256, :] = jnp.zeros((96, HID), BF)
    for j in range(2):
        wp[:, 128 * j : 128 * j + 128] = flat[pl.ds(OFF[3] + j, 1536, stride=2), :].astype(BF)
    for j in range(47):
        wo[:, 128 * j : 128 * j + 128] = flat[pl.ds(OFF[4] + j, 256, stride=47), :].astype(BF)
    wo[:, 6016:] = jnp.zeros((256, 128), BF)
    lane = lax.broadcasted_iota(jnp.int32, (768, 128), 1)
    a = [flat[pl.ds(OFF[1] + q, 768, stride=5), :] for q in range(5)]

    def put(r, t0, t1):
        tall[pl.ds(r, 768, stride=4), :] = t0
        tall2[pl.ds(r, 768, stride=4), :] = jnp.where(lane < 32, t1, 0.0)

    put(0, a[0], a[1])
    for r in (1, 2, 3):
        turn = 128 - 32 * r
        low = pltpu.roll(a[r], turn, 1)
        high = pltpu.roll(a[r + 1], turn, 1)
        put(r, jnp.where(lane < turn, low, high), high)
    for out, first in ((w1a, 0), (w1b, 1536)):
        out[:, 0:128] = tall[first : first + 1536, :].astype(BF)
        out[:, 128:256] = tall2[first : first + 1536, :].astype(BF)


def unpack(me, arrs):
    outs = (
        shape((256, HID), BF),
        shape((HID, 256), BF),
        shape((HID, 256), BF),
        shape((256, HID), BF),
        shape((256, HID), BF),
        shape((HID, PRE), BF),
        shape((PRE, SENP), BF),
    )
    return pl.pallas_call(
        unpack_kernel,
        out_shape=outs,
        in_specs=[SM] + [ANY] * 8,
        out_specs=(VM,) * 7,
        scratch_shapes=[
            pltpu.VMEM((32, BLK, 128), BF),
            pltpu.VMEM((ROWS_ALL + 64, 128), F32),
            pltpu.VMEM((3072, 128), F32),
            pltpu.VMEM((3072, 128), F32),
            pltpu.SemaphoreType.DMA((32,)),
        ],
        compiler_params=params(),
        name="unpack",
    )(me, *arrs)


def pack_kernel(me, gin, g1a, g1b, g2a, g2b, gp, go, keep, send, flat, tall, tall2):
    for j in range(12):
        flat[pl.ds(j, 220, stride=12), :] = gin[0:220, 128 * j : 128 * j + 128]
    for out, first in ((g1a, 0), (g1b, 1536)):
        tall[first : first + 1536, :] = out[:, 0:128]
        tall2[first : first + 1536, :] = out[:, 128:256]
    lane = lax.broadcasted_iota(jnp.int32, (768, 128), 1)
    t0 = [tall[pl.ds(r, 768, stride=4), :] for r in range(4)]
    t1 = [tall2[pl.ds(r, 768, stride=4), :] for r in range(4)]
    flat[pl.ds(OFF[1], 768, stride=5), :] = t0[0]
    for q in (1, 2, 3):
        tail = t1[q - 1] if q == 1 else jnp.where(
            lane < 32 * (q - 1), pltpu.roll(t0[q - 1], 32 * (q - 1), 1), pltpu.roll(t1[q - 1], 32 * (q - 1), 1)
        )
        flat[pl.ds(OFF[1] + q, 768, stride=5), :] = jnp.where(
            lane < 32 * q, tail, pltpu.roll(t0[q], 32 * q, 1)
        )
    flat[pl.ds(OFF[1] + 4, 768, stride=5), :] = jnp.where(
        lane < 96, pltpu.roll(t0[3], 96, 1), pltpu.roll(t1[3], 96, 1)
    )
    for j in range(12):
        flat[pl.ds(OFF[2] + j, 160, stride=12), :] = g2a[0:160, 128 * j : 128 * j + 128]
        flat[pl.ds(OFF[2] + 1920 + j, 160, stride=12), :] = g2b[0:160, 128 * j : 128 * j + 128]
    for j in range(2):
        flat[pl.ds(OFF[3] + j, 1536, stride=2), :] = gp[:, 128 * j : 128 * j + 128]
    for j in range(47):
        flat[pl.ds(OFF[4] + j, 256, stride=47), :] = go[:, 128 * j : 128 * j + 128].astype(F32)
    for dc, out in ((0, keep), (1, send)):
        for r in range(4):
            for j in range(4):
                z = lax.rem(me[0] + r, 4)
                y = me[1] ^ (j >> 1)
                x = me[2] ^ (j & 1)
                c = me[3] ^ dc
                base = ((z * 2 + y) * 2 + x) * CHIP + c * 794
                out[r, j] = flat[pl.ds(base, BLK), :].astype(BF)


def pack(me, *grads):
    return pl.pallas_call(
        pack_kernel,
        out_shape=(shape((4, 4, BLK, 128), BF),) * 2,
        in_specs=[SM] + [VM] * 7,
        out_specs=(VM,) * 2,
        scratch_shapes=[
            pltpu.VMEM((ROWS_ALL + 64, 128), F32),
            pltpu.VMEM((3072, 128), F32),
            pltpu.VMEM((3072, 128), F32),
        ],
        compiler_params=params(),
        name="pack",
    )(me, *grads)


def gelu_parts(act):
    square = act * act
    t = jnp.tanh(GELU_C * act * (1.0 + 0.044715 * square))
    cdf = 0.5 + 0.5 * t
    slope = cdf + (0.5 * act) * (1.0 - t * t) * (GELU_C + (3 * 0.044715 * GELU_C) * square)
    return act * cdf, slope


def put_sums(st, first, v):
    for s, (a, b) in enumerate(SEGS):
        st[first + s : first + s + 1, :] = jnp.sum(v[a:b], axis=0, keepdims=True)


def norm_rows(tot, s, cols):
    count = tot[6:7, s : s + 1]
    mean = tot[s : s + 1, cols] / count
    var = tot[3 + s : 4 + s, cols] / count - mean * mean
    return mean, lax.rsqrt(var + norm_eps)


def put_stats(st, hidden, mask):
    masked = hidden * mask
    put_sums(st, 0, masked)
    put_sums(st, 3, masked * hidden)
    lane = lax.broadcasted_iota(jnp.int32, (2, TILE), 1)
    counts = [jnp.sum(mask[a:b], axis=0, keepdims=True) for a, b in SEGS]
    st[6:8, :] = jnp.where(lane == 0, counts[0], jnp.where(lane == 1, counts[1], counts[2]))


def in_kernel(spl, w, b, rowm, h, gp, st):
    act = dot(spl[...], w[...]) + b[...]
    hidden, slope = gelu_parts(act)
    h[...] = hidden
    gp[...] = slope
    put_stats(st, hidden, rowm[:, 0:1])


def layer_in(spliced, w_in, b_in, rowm):
    col = lambda rows: pl.BlockSpec((rows, TILE), lambda i: (0, i))
    full = lambda c: pl.BlockSpec((ROWS, c), lambda i: (0, 0))
    return pl.pallas_call(
        in_kernel,
        grid=(NT,),
        out_shape=(shape((ROWS, HID)), shape((ROWS, HID)), shape((8, HID))),
        in_specs=[full(256), col(256), col(1), full(8)],
        out_specs=(col(ROWS), col(ROWS), col(8)),
        compiler_params=params(),
        name="layer_in",
    )(spliced, w_in, b_in, rowm)


def mid_kernel(h, tot, w1a, w1b, w2a, w2b, b2, rowm, rounded, fac, fnext, h2, gp2, st, ua, ub):
    i = pl.program_id(0)
    valid = rowm[:, 2:3]

    @pl.when(i < NT)
    def _():
        cols = at(i, TILE)
        for s, (a, b) in enumerate(SEGS):
            mean, scale = norm_rows(tot, s, cols)
            rounded[a:b, :] = ((h[a:b, :] - mean) * scale).astype(BF)
        pa = dot(rounded[...], w1a[...])
        pb = dot(rounded[...], w1b[...])

        @pl.when(i == 0)
        def _():
            ua[...] = pa
            ub[...] = pb

        @pl.when(i > 0)
        def _():
            ua[...] += pa
            ub[...] += pb

        @pl.when(i == NT - 1)
        def _():
            f = ((ub[...] + pltpu.roll(ua[...] * valid, 1, 0)) * valid).astype(BF)
            fac[...] = f
            fnext[...] = (pltpu.roll(f.astype(F32), ROWS - 1, 0) * valid).astype(BF)

    @pl.when(i >= NT)
    def _():
        act = dot(fac[...], w2a[...]) + dot(fnext[...], w2b[...]) + b2[...]
        hidden, slope = gelu_parts(act)
        h2[...] = hidden
        gp2[...] = slope
        put_stats(st, hidden, rowm[:, 0:1])


def layer_mid(h, tot, w1a, w1b, w2a, w2b, b2, rowm):
    first = lambda i: jnp.minimum(i, NT - 1)
    second = lambda i: jnp.maximum(i - NT, 0)
    fcol = lambda rows: pl.BlockSpec((rows, TILE), lambda i: (0, first(i)))
    scol = lambda rows: pl.BlockSpec((rows, TILE), lambda i: (0, second(i)))
    frow = pl.BlockSpec((TILE, 256), lambda i: (first(i), 0))
    full = lambda r, c: pl.BlockSpec((r, c), lambda i: (0, 0))
    return pl.pallas_call(
        mid_kernel,
        grid=(2 * NT,),
        out_shape=(
            shape((ROWS, HID), BF),
            shape((ROWS, 256), BF),
            shape((ROWS, 256), BF),
            shape((ROWS, HID)),
            shape((ROWS, HID)),
            shape((8, HID)),
        ),
        in_specs=[fcol(ROWS), full(8, HID), frow, frow, scol(256), scol(256), scol(1), full(ROWS, 8)],
        out_specs=(fcol(ROWS), full(ROWS, 256), full(ROWS, 256), scol(ROWS), scol(ROWS), scol(8)),
        scratch_shapes=[pltpu.VMEM((ROWS, 256), F32)] * 2,
        compiler_params=params(),
        name="layer_mid",
    )(h, tot, w1a, w1b, w2a, w2b, b2, rowm)


def head_kernel(
    h1, tot1, h2, tot2, wp, bp, wo, bo, rowm, summed, dpre, dsum, go, gb, st, loss, lg, acc, run, run2
):
    acc[...] = jnp.zeros_like(acc)

    @pl.loop(0, NT)
    def _(j):
        cols = at(j, TILE)
        for s, (a, b) in enumerate(SEGS):
            mean1, scale1 = norm_rows(tot1, s, cols)
            mean2, scale2 = norm_rows(tot2, s, cols)
            n1 = (h1[a:b, cols] - mean1) * scale1
            n2 = (h2[a:b, cols] - mean2) * scale2
            summed[a:b, cols] = (n2 + bypass_scale * n1).astype(BF)
        acc[...] += dot(summed[:, cols], wp[cols, :])

    pre = (acc[...] + bp[...]).astype(BF)
    run[...] = jnp.full_like(run, -jnp.inf)

    @pl.loop(0, NW)
    def _(j):
        v = dot(pre, wo[:, at(j, WIDE)]) + bo[:, at(j, WIDE)]
        lg[j] = v
        m = run[...]
        for q in range(WIDE // 128):
            m = jnp.maximum(m, v[:, 128 * q : 128 * q + 128])
        run[...] = m

    top = jnp.max(run[...], axis=1, keepdims=True)
    lane = lax.broadcasted_iota(jnp.int32, (ROWS, 128), 1)
    where = rowm[:, 3:4].astype(jnp.int32) - lane
    weight = rowm[:, 1:2]
    run[...] = jnp.zeros_like(run)
    run2[...] = jnp.zeros_like(run2)

    @pl.loop(0, NW)
    def _(j):
        total = run[...]
        picked = run2[...]
        for q in range(WIDE // 128):
            v = lg[j, :, 128 * q : 128 * q + 128]
            e = jnp.exp(v - top)
            lg[j, :, 128 * q : 128 * q + 128] = e
            total = total + e
            picked = picked + jnp.where(where == j * WIDE + 128 * q, v, 0.0)
        run[...] = total
        run2[...] = picked

    total = jnp.sum(run[...], axis=1, keepdims=True)
    picked = jnp.sum(run2[...], axis=1, keepdims=True)
    lse = jnp.log(total) + top
    loss[...] = jnp.zeros((8, 128), F32) + jnp.sum(weight * (lse - picked), axis=0, keepdims=True)
    ratio = weight / total
    acc[...] = jnp.zeros_like(acc)
    pre_t = pre.astype(F32).T.astype(BF)
    ones = jnp.ones((16, ROWS), BF)

    @pl.loop(0, NW)
    def _(j):
        parts = []
        for q in range(WIDE // 128):
            e = lg[j, :, 128 * q : 128 * q + 128]
            parts.append((e * ratio - jnp.where(where == j * WIDE + 128 * q, weight, 0.0)).astype(BF))
        d = jnp.concatenate(parts, axis=1)
        acc[...] += dot_nt(d, wo[:, at(j, WIDE)])
        go[:, at(j, WIDE)] = dot(pre_t, d).astype(BF)
        gb[:, at(j, WIDE)] = dot(ones, d)[0:8]

    dp = acc[...].astype(BF)
    dpre[...] = dp

    @pl.loop(0, NT)
    def _(j):
        cols = at(j, TILE)
        ds = dot_nt(dp, wp[cols, :])
        dsum[:, cols] = ds
        for s, (a, b) in enumerate(SEGS):
            mean2, scale2 = norm_rows(tot2, s, cols)
            n2 = (h2[a:b, cols] - mean2) * scale2
            st[s : s + 1, cols] = jnp.sum(ds[a:b], axis=0, keepdims=True)
            st[3 + s : 4 + s, cols] = jnp.sum(ds[a:b] * n2, axis=0, keepdims=True)

    st[6:8, :] = jnp.zeros((2, HID), F32)


def head(h1, tot1, h2, tot2, wp, bp, wo, bo, rowm):
    return pl.pallas_call(
        head_kernel,
        out_shape=(
            shape((ROWS, HID), BF),
            shape((ROWS, PRE), BF),
            shape((ROWS, HID)),
            shape((PRE, SENP), BF),
            shape((8, SENP)),
            shape((8, HID)),
            shape((8, 128)),
        ),
        in_specs=[VM] * 9,
        out_specs=(VM,) * 7,
        scratch_shapes=[
            pltpu.VMEM((NW, ROWS, WIDE), F32),
            pltpu.VMEM((ROWS, PRE), F32),
            pltpu.VMEM((ROWS, 128), F32),
            pltpu.VMEM((ROWS, 128), F32),
        ],
        compiler_params=params(62),
        name="head",
    )(h1, tot1, h2, tot2, wp, bp, wo, bo, rowm)


def back_mid_kernel(
    h1, tot1, h2, gp2, tot2, dsum, tot3, w1a, w1b, w2a, w2b, rowm, dact, dfac, dfnext, dn, st, ua, ub
):
    i = pl.program_id(0)
    valid = rowm[:, 2:3]

    @pl.when(i < NT)
    def _():
        cols = at(i, TILE)
        for s, (a, b) in enumerate(SEGS):
            mean, scale = norm_rows(tot2, s, cols)
            along = tot3[s : s + 1, cols]
            cross = tot3[3 + s : 4 + s, cols]
            part = rowm[a:b, 0:1] / tot1[6:7, s : s + 1]
            n2 = (h2[a:b, :] - mean) * scale
            back = scale * (dsum[a:b, :] - part * (along + cross * n2))
            dact[a:b, :] = (gp2[a:b, :] * back).astype(BF)
        pa = dot_nt(dact[...], w2a[...])
        pb = dot_nt(dact[...], w2b[...])

        @pl.when(i == 0)
        def _():
            ua[...] = pa
            ub[...] = pb

        @pl.when(i > 0)
        def _():
            ua[...] += pa
            ub[...] += pb

        @pl.when(i == NT - 1)
        def _():
            f = ((ua[...] + pltpu.roll(ub[...], 1, 0)) * valid).astype(BF)
            dfac[...] = f
            dfnext[...] = (pltpu.roll(f.astype(F32), ROWS - 1, 0) * valid).astype(BF)

    @pl.when(i >= NT)
    def _():
        cols = at(i - NT, TILE)
        grad = bypass_scale * dsum[...] + dot_nt(dfac[...], w1b[...]) + dot_nt(dfnext[...], w1a[...])
        dn[...] = grad
        for s, (a, b) in enumerate(SEGS):
            mean, scale = norm_rows(tot1, s, cols)
            n1 = (h1[a:b, :] - mean) * scale
            st[s : s + 1, :] = jnp.sum(grad[a:b], axis=0, keepdims=True)
            st[3 + s : 4 + s, :] = jnp.sum(grad[a:b] * n1, axis=0, keepdims=True)
        st[6:8, :] = jnp.zeros((2, TILE), F32)


def back_mid(h1, tot1, h2, gp2, tot2, dsum, tot3, w1a, w1b, w2a, w2b, rowm):
    first = lambda i: jnp.minimum(i, NT - 1)
    second = lambda i: jnp.maximum(i - NT, 0)
    fcol = lambda rows: pl.BlockSpec((rows, TILE), lambda i: (0, first(i)))
    scol = lambda rows: pl.BlockSpec((rows, TILE), lambda i: (0, second(i)))
    both = pl.BlockSpec((ROWS, TILE), lambda i: (0, lax.rem(i, NT)))
    srow = pl.BlockSpec((TILE, 256), lambda i: (second(i), 0))
    full = lambda r, c: pl.BlockSpec((r, c), lambda i: (0, 0))
    return pl.pallas_call(
        back_mid_kernel,
        grid=(2 * NT,),
        out_shape=(
            shape((ROWS, HID), BF),
            shape((ROWS, 256), BF),
            shape((ROWS, 256), BF),
            shape((ROWS, HID)),
            shape((8, HID)),
        ),
        in_specs=[
            scol(ROWS),
            full(8, HID),
            fcol(ROWS),
            fcol(ROWS),
            full(8, HID),
            both,
            full(8, HID),
            srow,
            srow,
            fcol(256),
            fcol(256),
            full(ROWS, 8),
        ],
        out_specs=(fcol(ROWS), full(ROWS, 256), full(ROWS, 256), scol(ROWS), scol(8)),
        scratch_shapes=[pltpu.VMEM((ROWS, 256), F32)] * 2,
        compiler_params=params(),
        name="back_mid",
    )(h1, tot1, h2, gp2, tot2, dsum, tot3, w1a, w1b, w2a, w2b, rowm)


def side_kernel(summed, dpre, fac, fnext, dact, rounded, dfac, dfnext, g1a, g1b, g2a, g2b, gp, gbp, gbs):
    fac_t = fac[...].astype(F32).T.astype(BF)
    next_t = fnext[...].astype(F32).T.astype(BF)
    ones = jnp.ones((16, ROWS), BF)
    gbp[...] = dot(ones, dpre[...])[0:8]

    @pl.loop(0, NT)
    def _(j):
        cols = at(j, TILE)
        t = summed[:, cols].astype(F32).T.astype(BF)
        gp[cols, :] = dot(t, dpre[...])
        t = rounded[:, cols].astype(F32).T.astype(BF)
        g1a[cols, :] = dot(t, dfnext[...])
        g1b[cols, :] = dot(t, dfac[...])
        g2a[:, cols] = dot(fac_t, dact[:, cols])
        g2b[:, cols] = dot(next_t, dact[:, cols])
        gbs[:, cols] = dot(ones, dact[:, cols])[0:8]


def side(*args):
    return pl.pallas_call(
        side_kernel,
        out_shape=(
            shape((HID, 256)),
            shape((HID, 256)),
            shape((256, HID)),
            shape((256, HID)),
            shape((HID, PRE)),
            shape((8, PRE)),
            shape((8, HID)),
        ),
        in_specs=[VM] * 8,
        out_specs=(VM,) * 7,
        compiler_params=params(),
        name="side",
    )(*args)


def back_in_kernel(h1, gp, tot1, dn, tot4, spl_t, rowm, gin):
    i = pl.program_id(0)
    cols = at(i, TILE)
    parts = []
    for s, (a, b) in enumerate(SEGS):
        mean, scale = norm_rows(tot1, s, cols)
        along = tot4[s : s + 1, cols]
        cross = tot4[3 + s : 4 + s, cols]
        part = rowm[a:b, 0:1] / tot1[6:7, s : s + 1]
        n1 = (h1[a:b, :] - mean) * scale
        back = scale * (dn[a:b, :] - part * (along + cross * n1))
        parts.append((gp[a:b, :] * back).astype(BF))
    gin[...] = dot(spl_t[...], jnp.concatenate(parts, axis=0))


def back_in(h1, gp, tot1, dn, tot4, spl_t, rowm):
    col = lambda rows: pl.BlockSpec((rows, TILE), lambda i: (0, i))
    full = lambda r, c: pl.BlockSpec((r, c), lambda i: (0, 0))
    return pl.pallas_call(
        back_in_kernel,
        grid=(NT,),
        out_shape=shape((256, HID)),
        in_specs=[col(ROWS), col(ROWS), full(8, HID), col(ROWS), full(8, HID), full(256, ROWS), full(ROWS, 8)],
        out_specs=col(256),
        compiler_params=params(),
        name="back_in",
    )(h1, gp, tot1, dn, tot4, spl_t, rowm)


def move(x, n, mask):
    return lax.ppermute(x, "dp", [(i, i ^ mask) for i in range(n)])


def turn(x, n, layers):
    return lax.ppermute(x, "dp", [(i, (i + 8 * layers) % n) for i in range(n)])


def total(x, n):
    bit = 1
    while bit < n:
        if bit > 1 and 2 * bit < n:
            a, b, c = move(x, n, bit), move(x, n, 2 * bit), move(x, n, 3 * bit)
            x = (x + a) + (b + c)
            bit = 4 * bit
        else:
            x = x + move(x, n, bit)
            bit = 2 * bit
    return x


def fits(n, shard):
    return n == 32 and 2 * shard == CHIP * 128


def gather_blocks(shard, n, me):
    size = shard.shape[0]
    if fits(n, size):
        own = lax.dynamic_update_slice(jnp.zeros((BLK * 128,), BF), shard, (64 * me[3],)).reshape(BLK, 128)
        near, far = [], []
        for layer in LAYERS:
            v = own if layer == 0 else turn(own, n, layer)
            vx, vy = move(v, n, 2), move(v, n, 4)
            half = BLK // 2
            vxy = jnp.concatenate([move(vx[:half], n, 4), move(vy[half:], n, 2)], axis=0)
            stack = jnp.stack([v, vx, vy, vxy])
            near.append(stack)
            far.append(move(stack, n, 1))
        return near + far
    flat = lax.all_gather(shard, "dp", axis=0, tiled=True).reshape(16, CHIP, 128)
    lane = jnp.arange(128)[None, None, :]
    row = jnp.arange(795)[None, :, None]
    even = jnp.where((row == 794) & (lane >= 64), 0, flat[:, :795])
    odd = jnp.where((row == 0) & (lane < 64), 0, flat[:, 794:])
    blocks = jnp.pad(jnp.stack([even, odd], axis=1), ((0, 0), (0, 0), (0, BLK - 795), (0, 0)))
    blocks = blocks.reshape(4, 4, 2, BLK, 128)
    return [blocks[(4 - layer) % 4, :, c] for c in (0, 1) for layer in LAYERS]


def scatter_sum(keep, send, n, me, size):
    if fits(n, size):
        half = BLK // 2
        v = keep + move(send, n, 1)
        a, b = v[:, :, :half], v[:, :, half:]
        a = a[:, 0::2] + move(a[:, 1::2], n, 2)
        b = b[:, :2] + move(b[:, 2:], n, 4)
        a = a[:, 0] + move(a[:, 1], n, 4)
        b = b[:, 0] + move(b[:, 1], n, 2)
        v = jnp.concatenate([a, b], axis=1)
        out = v[0].astype(F32)
        for r in (1, 2, 3):
            out = out + turn(v[r], n, r).astype(F32)
        return lax.dynamic_slice(out.reshape(-1), (64 * me[3],), (size,))
    even = keep.reshape(16, BLK, 128)[:, :794]
    odd = send.reshape(16, BLK, 128)[:, :795]
    flat = jnp.concatenate([even, odd], axis=1).reshape(n, size)
    return lax.psum_scatter(flat.astype(F32), "dp", scatter_dimension=0, tiled=True).reshape(-1)


def adam(value, grad, first, second, decay):
    first = beta_one * first + (1.0 - beta_one) * grad
    second = beta_two * second + (1.0 - beta_two) * grad * grad
    first_hat = first / (1.0 - beta_one**STEP)
    second_hat = second / (1.0 - beta_two**STEP)
    value = value - learn_rate * (first_hat / (jnp.sqrt(second_hat) + adam_eps) + decay * value)
    return (value, first, second)


def pad_rows(v):
    parts = []
    at_row = 0
    for k, length in enumerate(SPAN):
        parts.append(v[at_row : at_row + length])
        end = START[k + 1] if k + 1 < len(START) else ROWS
        parts.append(jnp.zeros((end - START[k] - length,) + v.shape[1:], v.dtype))
        at_row = at_row + length
    return jnp.concatenate(parts, axis=0)


def on_device(
    features,
    ivectors,
    frame_mask,
    labels,
    confidence,
    weights,
    first_moment,
    second_moment,
    biases,
    bias_first,
    bias_second,
):
    n = lax.axis_size("dp")
    size = weights.shape[1]
    index = lax.axis_index("dp")
    if fits(n, size):
        me = jnp.stack([index // 8, (index // 4) % 2, (index // 2) % 2, index % 2]).astype(jnp.int32)
    else:
        me = jnp.zeros((4,), jnp.int32)
    arrs = gather_blocks(weights.astype(BF).reshape(-1), n, me)
    w_in, w1a, w1b, w2a, w2b, w_pre, w_out = unpack(me, arrs)
    b_in = biases[None, :HID]
    b_second = biases[None, HID : 2 * HID]
    b_pre = biases[None, 2 * HID : 2 * HID + PRE]
    b_out = jnp.pad(biases[None, 2 * HID + PRE :], ((0, 0), (0, SENP - SEN)), constant_values=-1e30)

    mask = frame_mask.astype(F32)
    weight = confidence * mask
    meta = jnp.stack([mask, weight, jnp.ones_like(mask), labels.astype(F32)] + [jnp.zeros_like(mask)] * 4, axis=1)
    rowm = pad_rows(meta)
    valid = rowm[:, 2:3].astype(BF)
    feats = pad_rows(features)
    gap = jnp.zeros((1, FEAT), BF)
    before = jnp.concatenate([gap, feats[:-1]], axis=0)
    after = jnp.concatenate([feats[1:], gap], axis=0)
    wide = pad_rows(jnp.concatenate([jnp.broadcast_to(ivectors[k : k + 1], (SPAN[k], IVEC)) for k in range(4)], axis=0))
    spliced = jnp.concatenate(
        [before, feats, after, wide, valid, jnp.zeros((ROWS, 256 - 3 * FEAT - IVEC - 1), BF)], axis=1
    )
    spl_t = spliced.T

    h1, gp1, st = layer_in(spliced, w_in, b_in, rowm)
    tot1 = total(st, n)
    rounded, fac, fnext, h2, gp2, st = layer_mid(h1, tot1, w1a, w1b, w2a, w2b, b_second, rowm)
    tot2 = total(st, n)
    summed, dpre, dsum, go, gbo, st, loss = head(h1, tot1, h2, tot2, w_pre, b_pre, w_out, b_out, rowm)
    tot3 = total(st, n)
    dact, dfac, dfnext, dn, st = back_mid(h1, tot1, h2, gp2, tot2, dsum, tot3, w1a, w1b, w2a, w2b, rowm)
    tot4 = total(st, n)
    g1a, g1b, g2a, g2b, gpre, gbp, gbs = side(summed, dpre, fac, fnext, dact, rounded, dfac, dfnext)
    gin = back_in(h1, gp1, tot1, dn, tot4, spl_t, rowm)
    keep, send = pack(me, gin, g1a, g1b, g2a, g2b, gpre, go)
    grad = scatter_sum(keep, send, n, me, size)

    bias_grad = jnp.concatenate([gin[220], gbs[0], gbp[0], gbo[0, :SEN]])
    extra = jnp.stack([jnp.sum(grad * grad), loss[0, 0], jnp.sum(weight)])
    last = total(jnp.concatenate([bias_grad, jnp.pad(extra, (0, 7 * 128 - 3))]).reshape(80, 128), n).reshape(-1)
    bias_sum = last[:NBIAS]
    squares, loss_sum, loss_weight = last[NBIAS], last[NBIAS + 1], last[NBIAS + 2]
    grad_norm = jnp.sqrt(squares + jnp.sum(bias_sum * bias_sum))
    scale = jnp.minimum(jnp.float32(1.0), clip_norm / grad_norm)
    new_w, new_m, new_v = adam(weights, (grad * scale)[None], first_moment, second_moment, decay_rate)
    new_b, new_bm, new_bv = adam(biases, bias_sum * scale, bias_first, bias_second, 0.0)
    return (new_w, new_m, new_v, new_b, new_bm, new_bv, loss_sum, loss_weight, grad_norm)


def solution(mesh):
    return jax.shard_map(
        on_device,
        mesh=mesh,
        in_specs=(
            P("dp", None),
            P("dp", None),
            P("dp"),
            P("dp"),
            P("dp"),
            P("dp", None),
            P("dp", None),
            P("dp", None),
            P(),
            P(),
            P(),
        ),
        out_specs=(P("dp", None), P("dp", None), P("dp", None), P(), P(), P(), P(), P(), P()),
        check_vma=False,
    )
```

time: 1030 us -> 331 us (0.32)
  waiting for transfers between devices: 312 us -> 92.7 us
  blocking collectives: 205 us -> 0 us
  other arithmetic: 221 us -> 24.9 us
  local copies, waits for them, and re-layouts: 182 us -> 14.8 us
  Pallas kernels: 0 us -> 116 us
  matrix products: 78 us -> 0 us
  starting transfers between devices: 0.08 us -> 77.2 us
  between operations: 20.8 us -> 3.9 us
    unnamed x3 -> x0, waiting for transfers between devices: 232 us -> none
    psum x5 -> x0, blocking collectives: 205 us -> none  [the longest x2 82.2 us: normalize(): lax.psum((jnp.sum(wide * hidden, axis=0), jnp.sum(wide * hidden * hidden,...]
    all_gather x1 -> x0, other arithmetic: 136 us -> none  [on_device(): mats = unpack(lax.all_gather(shard, 'dp', axis=0, tiled=True).reshape(-1))]
    pallas_call x0 -> x8, Pallas kernels: none -> 116 us  [the longest x1 34.3 us: head(): pl.pallas_call(head_kernel, out_shape=(shape((ROWS, HID), BF), shape((ROW...]
    ppermute x0 -> x66, waiting for transfers between devices: none -> 92.7 us  [the longest x60 73.8 us: move(): return lax.ppermute(x, 'dp', [(i, i ^ mask) for i in range(n)])]
    all_gather x1 -> x0, waiting for transfers between devices: 80.4 us -> none  [on_device(): mats = unpack(lax.all_gather(shard, 'dp', axis=0, tiled=True).reshape(-1))]
    dot_general x42 -> x0, matrix products: 78 us -> none  [the longest x15 34 us: product_left(): lax.dot_general(left, right, (((0,), (0,)), ((), ())), preferred_element_...]
    ppermute x0 -> x66, starting transfers between devices: none -> 77.2 us  [the longest x60 67.2 us: move(): return lax.ppermute(x, 'dp', [(i, i ^ mask) for i in range(n)])]
  transfers between devices with their start and end apart: 2 -> 66, of which waited for: 2 -> 39; matrix products, arithmetic and copies ran while one was open for 2% -> 5% of each run, Pallas kernels for 0% -> 3%
where the time goes in v1:
time: 331 us; the launch traced here: 329 us
  Pallas kernels  116 us (35%)
  waiting for transfers between devices  92.7 us (28%)
  starting transfers between devices  77.2 us (23%)
  other arithmetic  24.9 us (8%)
  local copies, waits for them, and re-layouts  14.8 us (4%)
  between operations  3.9 us (1%)
    ppermute x60, waiting for transfers between devices, move(): return lax.ppermute(x, 'dp', [(i, i ^ mask) for i in range(n)])  73.8 us
    ppermute x60, starting transfers between devices, move(): return lax.ppermute(x, 'dp', [(i, i ^ mask) for i in range(n)])  67.2 us
    pallas_call x1, Pallas kernels, head(): pl.pallas_call(head_kernel, out_shape=(shape((ROWS, HID), BF), shape((ROW...  34.3 us
    ppermute x6, waiting for transfers between devices, turn(): return lax.ppermute(x, 'dp', [(i, (i + 8 * layers) % n) for i in range(n)])  18.9 us
    pallas_call x1, Pallas kernels, back_mid(): pl.pallas_call(back_mid_kernel, grid=(2 * NT,), out_shape=(shape((ROWS, H...  18.6 us
    pallas_call x1, Pallas kernels, layer_mid(): pl.pallas_call(mid_kernel, grid=(2 * NT,), out_shape=(shape((ROWS, HID),...  15.4 us
    pallas_call x1, Pallas kernels, side(): pl.pallas_call(side_kernel, out_shape=(shape((HID, 256)), shape((HID, 256...  11.4 us
    ppermute x6, starting transfers between devices, turn(): return lax.ppermute(x, 'dp', [(i, (i + 8 * layers) % n) for i in range(n)])  10 us
  transfers between devices with their start and end apart: 66, of which 39 were waited for; matrix products, arithmetic and copies ran while one was open for 5% of the time, Pallas kernels for 3%

profile of v1, /device:TPU:0, one launch (start us, length us, event | category | flops | bytes accessed | tf_op | source)
XLA Modules:
  0.0 329.4 jit_solution(14294085872064120972)
XLA Ops:
  4.8 4.1 %collective-permute-start.14 = (bf16[800,128]{1,0:T(8,128)(2,1)S(1)}, bf16[800,128]{1,0:T(8,128)(2,1)S(1)}, u32[]{:S(2)}, u32[]{:S(2)}) collective-permute-start(bf16[800,128]{1,0:T(8,128)(2,1)S(1)} %bitcast.82), channel_id=1, source_target_pairs={{0,16},{1,17},{2,18},{3,19},{4,20},{5,21},{6,22},{7,23},{8,24},{9,... | collective-permute-start | bytes 614408 | tf_op jit(solution)/shard_map/ppermute | solution.py:596
  20.0 3.9 %collective-permute-done.4 = bf16[800,128]{1,0:T(8,128)(2,1)S(1)} collective-permute-done((bf16[800,128]{1,0:T(8,128)(2,1)S(1)}, bf16[800,128]{1,0:T(8,128)(2,1)S(1)}, u32[]{:S(2)}, u32[]{:S(2)}) %collective-permute-start.4) | collective-permute-done | bytes 204832 | tf_op jit(solution)/shard_map/ppermute | solution.py:596
  45.0 2.6 collective-permute-done.13
  55.8 9.5 %unpack.1 = (bf16[256,1536]{1,0:T(8,128)(2,1)}, bf16[1536,256]{1,0:T(8,128)(2,1)}, bf16[1536,256]{1,0:T(8,128)(2,1)}, bf16[256,1536]{1,0:T(8,128)(2,1)}, bf16[25...) custom-call(s32[4]{0:T(128)} %pad_add_fusion.me, bf16[4,800,128]{2,1,0:T(8,128)(2,1)} %copy-done.1, ...), custom_call_target="tpu_custom_call" | custom-call | tf_op jit(solution)/shard_map/unpack/pallas_call | solution.py:140
  65.3 8.2 %layer_in.1 = (f32[768,1536]{1,0:T(8,128)}, f32[768,1536]{1,0:T(8,128)}, f32[8,1536]{1,0:T(8,128)}) custom-call(bf16[768,256]{1,0:T(8,128)(2,1)} %copy.39.spl, bf16[256,1536]{1,0:T(8,128)(2,1)} %get-tuple-element.46.w, f32[1,1536]{1,0:T(1,128)} %broadcast_in_dim.82.b, f32[768,8]{1,0:T(8,128)} %copy.40.rowm), custom_call_target="tpu_custom_call" | custom-call | tf_op jit(solution)/shard_map/layer_in/pallas_call | solution.py:251
  82.1 2.5 collective-permute-start.29
  84.5 4.8 %collective-permute-start.28 = (f32[8,1536]{1,0:T(8,128)S(1)}, f32[8,1536]{1,0:T(8,128)S(1)}, u32[]{:S(2)}, u32[]{:S(2)}) collective-permute-start(f32[8,1536]{1,0:T(8,128)S(1)} %add_add_fusion.7), channel_id=1, source_target_pairs={{0,16},{1,17},{2,18},{3,19},{4,20},{5,21},{6,22},{7,23},{8,24},{9,... | collective-permute-start | bytes 147464 | tf_op jit(solution)/shard_map/ppermute | solution.py:592
  94.1 15.4 %layer_mid.1 = (bf16[768,1536]{1,0:T(8,128)(2,1)}, bf16[768,256]{1,0:T(8,128)(2,1)}, bf16[768,256]{1,0:T(8,128)(2,1)}, f32[768,1536]{1,0:T(8,128)}, f32[768,1536]{1,0:T(8,128)}, /*index=5*/f32[8,1536]{1,0:T(8,128)}) custom-call(f32[768,1536]{1,0:T(8,128)} %get-tuple-element.47.h.h1, f32[8,1536]{1,0:T(8,128)} %add_add_fusion.6.tot.tot1, ...), custom_call_target="tpu_custom_call" | custom-call | tf_op jit(solution)/shard_map/layer_mid/pallas_call | solution.py:307
  118.9 2.9 collective-permute-start.36
  127.4 34.3 %head.1 = (bf16[768,1536]{1,0:T(8,128)(2,1)}, bf16[768,256]{1,0:T(8,128)(2,1)}, f32[768,1536]{1,0:T(8,128)}, bf16[256,6144]{1,0:T(8,128)(2,1)}, f32[8,6144]{1,0:...) custom-call(f32[768,1536]{1,0:T(8,128)} %get-tuple-element.47.h.h1, f32[8,1536]{1,0:T(8,128)} %add_add_fusion.6.tot.tot1, ...), custom_call_target="tpu_custom_call" | custom-call | tf_op jit(solution)/shard_map/head/pallas_call | solution.py:412
  178.2 18.6 %back_mid.1 = (bf16[768,1536]{1,0:T(8,128)(2,1)}, bf16[768,256]{1,0:T(8,128)(2,1)}, bf16[768,256]{1,0:T(8,128)(2,1)}, f32[768,1536]{1,0:T(8,128)}, f32[8,1536]{1,0:T(8,128)}) custom-call(f32[768,1536]{1,0:T(8,128)} %get-tuple-element.47.h.h1, f32[8,1536]{1,0:T(8,128)} %add_add_fusion.6.tot.tot1, f32[768,1536]{1,0:T(8,128)} %get-tuple-element.54.h2, ...), custom_call_target="tpu_custom_call" | custom-call | tf_op jit(solution)/shard_map/back_mid/pallas_call | solution.py:493
  210.7 11.4 %side.1 = (f32[1536,256]{1,0:T(8,128)}, f32[1536,256]{1,0:T(8,128)}, f32[256,1536]{1,0:T(8,128)}, f32[256,1536]{1,0:T(8,128)}, f32[1536,256]{1,0:T(8,128)}, /*index=5*/f32[8,256]{1,0:T(8,128)}, f32[8,1536]{1,0:T(8,128)}) custom-call(bf16[768,1536]{1,0:T(8,128)(2,1)} %get-tuple-element.63.summed, bf16[768,256]{1,0:T(8,128)(2,1)} %get-tuple-element.64.dpre, ...), custom_call_target="tpu_custom_call" | custom-call | tf_op jit(solution)/shard_map/side/pallas_call | solution.py:544
  222.8 9.0 %back_in.1.gin = f32[256,1536]{1,0:T(8,128)} custom-call(f32[768,1536]{1,0:T(8,128)} %get-tuple-element.47.h.h1, f32[768,1536]{1,0:T(8,128)} %get-tuple-element.48.gp, f32[8,1536]{1,0:T(8,128)} %add_add_fusion.6.tot.tot1, f32[768,1536]{1,0:T(8,128)} %get-tuple-element.61.dn, f32[8,1536]{1,0:T(8,128)} %add_add_fusion.tot4, bf16[256,768]{1,0:T(8,128)(2,1)} %bitcast.81, ...), custom_call_target="tpu_custom_call" | custom-call | tf_op jit(solution)/shard_map/back_in/pallas_call | solution.py:580
  231.8 9.4 %pack.1 = (bf16[4,4,800,128]{3,2,1,0:T(8,128)(2,1)}, bf16[4,4,800,128]{3,2,1,0:T(8,128)(2,1)}) custom-call(s32[4]{0:T(128)} %pad_add_fusion.me, f32[256,1536]{1,0:T(8,128)} %back_in.1.gin, f32[1536,256]{1,0:T(8,128)} %get-tuple-element.71.g1a, f32[1536,256]{1,0:T(8,128)} %get-tuple-element.72.g1b, f32[256,1536]{1,0:T(8,128)} %get-tuple-element.73.g2a, ...), custom_call_target="tpu_custom_call" | custom-call | tf_op jit(solution)/shard_map/pack/pallas_call | solution.py:196
  241.2 6.1 %collective-permute-done.51 = bf16[4,4,800,128]{3,2,1,0:T(8,128)(2,1)S(1)} collective-permute-done((bf16[4,4,800,128]{3,2,1,0:T(8,128)(2,1)}, bf16[4,4,800,128]{3,2,1,0:T(8,128)(2,1)S(1)}, u32[]{:S(2)}, u32[]{:S(2)}) %collective-permute-start.51) | collective-permute-done | bytes 3276832 | tf_op jit(solution)/shard_map/ppermute | solution.py:592
  247.3 2.8 add.219
  256.7 14.9 %collective-permute-done.54 = bf16[4,2,400,128]{3,2,1,0:T(8,128)(2,1)} collective-permute-done((bf16[4,2,400,128]{3,2,1,0:T(8,128)(2,1)}, bf16[4,2,400,128]{3,2,1,0:T(8,128)(2,1)}, u32[]{:S(2)}, u32[]{:S(2)}) %collective-permute-start.54) | collective-permute-done | bytes 819232 | tf_op jit(solution)/shard_map/ppermute | solution.py:592
  274.0 9.7 %collective-permute-done.55 = bf16[4,400,128]{2,1,0:T(8,128)(2,1)S(1)} collective-permute-done((bf16[4,400,128]{2,1,0:T(8,128)(2,1)S(1)}, bf16[4,400,128]{2,1,0:T(8,128)(2,1)S(1)}, u32[]{:S(2)}, u32[]{:S(2)}) %collective-permute-start.55) | collective-permute-done | bytes 409632 | tf_op jit(solution)/shard_map/ppermute | solution.py:592
  284.4 3.7 %collective-permute-start.58 = (bf16[800,128]{1,0:T(8,128)(2,1)S(1)}, bf16[800,128]{1,0:T(8,128)(2,1)S(1)}, u32[]{:S(2)}, u32[]{:S(2)}) collective-permute-start(bf16[800,128]{1,0:T(8,128)(2,1)S(1)} %get-tuple-element.94), channel_id=1, source_target_pairs={{0,24},{1,25},{2,26},{3,27},{4,28},{5,29},{6,30},{7,31},{8,0},{9,1... | collective-permute-start | bytes 614408 | tf_op jit(solution)/shard_map/ppermute | solution.py:596
  288.1 6.1 %collective-permute-done.56 = bf16[800,128]{1,0:T(8,128)(2,1)S(1)} collective-permute-done((bf16[800,128]{1,0:T(8,128)(2,1)S(1)}, bf16[800,128]{1,0:T(8,128)(2,1)S(1)}, u32[]{:S(2)}, u32[]{:S(2)}) %collective-permute-start.56) | collective-permute-done | bytes 204832 | tf_op jit(solution)/shard_map/ppermute | solution.py:596
  294.2 8.9 %collective-permute-done.57 = bf16[800,128]{1,0:T(8,128)(2,1)S(1)} collective-permute-done((bf16[800,128]{1,0:T(8,128)(2,1)S(1)}, bf16[800,128]{1,0:T(8,128)(2,1)S(1)}, u32[]{:S(2)}, u32[]{:S(2)}) %collective-permute-start.57) | collective-permute-done | bytes 204832 | tf_op jit(solution)/shard_map/ppermute | solution.py:596
  307.9 2.3 collective-permute-start.62
  315.9 2.8 collective-permute-start.63
  324.6 3.7 %multiply_subtract_fusion = (f32[1,101696]{1,0:T(1,128)}, f32[1,101696]{1,0:T(1,128)}, f32[1,101696]{1,0:T(1,128)}) fusion(f32[1,101696]{1,0:T(1,128)S(1)} %copy-done.4, f32[101696]{0:T(1024)S(1)} %get-tuple-element.97, f32[1,101696]{1,0:T(1,128)S(1)} %copy-done.5, f32[101696]{0:T(1024)S(1)} %get-tuple-element.96, f32[1,101696]{1,0:T(1,128)S(1)} %copy-done.6), kind=kLoop, calls=%fused_computation.24 | loop fusion | flops 1220352 | bytes 3254272 | tf_op jit(solution)/shard_map/sub | solution.py:665
  (252 shorter events, 127.8 us)
Async XLA Ops:
  4.8 20.7 %collective-permute-start.14 = (bf16[800,128]{1,0:T(8,128)(2,1)S(1)}, bf16[800,128]{1,0:T(8,128)(2,1)S(1)}, u32[]{:S(2)}, u32[]{:S(2)}) collective-permute-start(bf16[800,128]{1,0:T(8,128)(2,1)S(1)} %bitcast.82), channel_id=1, source_target_pairs={{0,16},{1,17},{2,18},{3,19},{4,20},{5,21},{6,22},{7,23},{8,24},{9,... | collective-permute-start | bytes 614408 | tf_op jit(solution)/shard_map/ppermute | solution.py:596
  8.9 18.1 %collective-permute-start.9 = (bf16[800,128]{1,0:T(8,128)(2,1)S(1)}, bf16[800,128]{1,0:T(8,128)(2,1)S(1)}, u32[]{:S(2)}, u32[]{:S(2)}) collective-permute-start(bf16[800,128]{1,0:T(8,128)(2,1)S(1)} %bitcast.83), channel_id=1, source_target_pairs={{0,24},{1,25},{2,26},{3,27},{4,28},{5,29},{6,30},{7,31},{8,0},{9,1... | collective-permute-start | bytes 614408 | tf_op jit(solution)/shard_map/ppermute | solution.py:596
  10.2 13.7 %collective-permute-start.4 = (bf16[800,128]{1,0:T(8,128)(2,1)S(1)}, bf16[800,128]{1,0:T(8,128)(2,1)S(1)}, u32[]{:S(2)}, u32[]{:S(2)}) collective-permute-start(bf16[800,128]{1,0:T(8,128)(2,1)S(1)} %bitcast.84), channel_id=1, source_target_pairs={{0,8},{1,9},{2,10},{3,11},{4,12},{5,13},{6,14},{7,15},{8,16},{9,17... | collective-permute-start | bytes 614408 | tf_op jit(solution)/shard_map/ppermute | solution.py:596
  16.9 10.6 %collective-permute-start.3 = (bf16[400,128]{1,0:T(8,128)(2,1)S(1)}, bf16[400,128]{1,0:T(8,128)(2,1)S(1)}, u32[]{:S(2)}, u32[]{:S(2)}) collective-permute-start(bf16[400,128]{1,0:T(8,128)(2,1)S(1)} %slice.209), channel_id=1, source_target_pairs={{0,2},{1,3},{2,0},{3,1},{4,6},{5,7},{6,4},{7,5},{8,10},{9,11},{10,... | collective-permute-start | bytes 307208 | tf_op jit(solution)/shard_map/ppermute | solution.py:592
  18.5 9.6 %collective-permute-start.2 = (bf16[400,128]{1,0:T(8,128)(2,1)S(1)}, bf16[400,128]{1,0:T(8,128)(2,1)S(1)}, u32[]{:S(2)}, u32[]{:S(2)}) collective-permute-start(bf16[400,128]{1,0:T(8,128)(2,1)S(1)} %slice.208), channel_id=1, source_target_pairs={{0,4},{1,5},{2,6},{3,7},{4,0},{5,1},{6,2},{7,3},{8,12},{9,13},{10,... | collective-permute-start | bytes 307208 | tf_op jit(solution)/shard_map/ppermute | solution.py:592
  26.9 9.2 %collective-permute-start.16 = (bf16[800,128]{1,0:T(8,128)(2,1)S(1)}, bf16[800,128]{1,0:T(8,128)(2,1)S(1)}, u32[]{:S(2)}, u32[]{:S(2)}) collective-permute-start(bf16[800,128]{1,0:T(8,128)(2,1)S(1)} %collective-permute-done.14), channel_id=1, source_target_pairs={{0,4},{1,5},{2,6},{3,7},{4,0},{5,1},{6,2},{7,3},{8,12},{9,13},{10,... | collective-permute-start | bytes 614408 | tf_op jit(solution)/shard_map/ppermute | solution.py:592
  27.5 10.5 %collective-permute-start.15 = (bf16[800,128]{1,0:T(8,128)(2,1)S(1)}, bf16[800,128]{1,0:T(8,128)(2,1)S(1)}, u32[]{:S(2)}, u32[]{:S(2)}) collective-permute-start(bf16[800,128]{1,0:T(8,128)(2,1)S(1)} %collective-permute-done.14), channel_id=1, source_target_pairs={{0,2},{1,3},{2,0},{3,1},{4,6},{5,7},{6,4},{7,5},{8,10},{9,11},{10,... | collective-permute-start | bytes 614408 | tf_op jit(solution)/shard_map/ppermute | solution.py:592
  28.1 11.7 %collective-permute-start.11 = (bf16[800,128]{1,0:T(8,128)(2,1)S(1)}, bf16[800,128]{1,0:T(8,128)(2,1)S(1)}, u32[]{:S(2)}, u32[]{:S(2)}) collective-permute-start(bf16[800,128]{1,0:T(8,128)(2,1)S(1)} %collective-permute-done.9), channel_id=1, source_target_pairs={{0,4},{1,5},{2,6},{3,7},{4,0},{5,1},{6,2},{7,3},{8,12},{9,13},{10,... | collective-permute-start | bytes 614408 | tf_op jit(solution)/shard_map/ppermute | solution.py:592
  31.8 9.5 %collective-permute-start.10 = (bf16[800,128]{1,0:T(8,128)(2,1)S(1)}, bf16[800,128]{1,0:T(8,128)(2,1)S(1)}, u32[]{:S(2)}, u32[]{:S(2)}) collective-permute-start(bf16[800,128]{1,0:T(8,128)(2,1)S(1)} %collective-permute-done.9), channel_id=1, source_target_pairs={{0,2},{1,3},{2,0},{3,1},{4,6},{5,7},{6,4},{7,5},{8,10},{9,11},{10,... | collective-permute-start | bytes 614408 | tf_op jit(solution)/shard_map/ppermute | solution.py:592
  33.5 9.4 %collective-permute-start.8 = (bf16[400,128]{1,0:T(8,128)(2,1)S(1)}, bf16[400,128]{1,0:T(8,128)(2,1)S(1)}, u32[]{:S(2)}, u32[]{:S(2)}) collective-permute-start(bf16[400,128]{1,0:T(8,128)(2,1)S(1)} %slice.211), channel_id=1, source_target_pairs={{0,2},{1,3},{2,0},{3,1},{4,6},{5,7},{6,4},{7,5},{8,10},{9,11},{10,... | collective-permute-start | bytes 307208 | tf_op jit(solution)/shard_map/ppermute | solution.py:592
  38.0 17.8 %collective-permute-start.19 = (bf16[4,800,128]{2,1,0:T(8,128)(2,1)S(1)}, bf16[4,800,128]{2,1,0:T(8,128)(2,1)}, u32[]{:S(2)}, u32[]{:S(2)}) collective-permute-start(bf16[4,800,128]{2,1,0:T(8,128)(2,1)S(1)} %pad_maximum_fusion.refs_0_), channel_id=1, source_target_pairs={{0,1},{1,0},{2,3},{3,2},{4,5},{5,4},{6,7},{7,6},{8,9},{9,8},{10,11... | collective-permute-start | bytes 2457608 | tf_op jit(solution)/shard_map/ppermute | solution.py:592
  39.7 9.5 %collective-permute-start.18 = (bf16[400,128]{1,0:T(8,128)(2,1)S(1)}, bf16[400,128]{1,0:T(8,128)(2,1)S(1)}, u32[]{:S(2)}, u32[]{:S(2)}) collective-permute-start(bf16[400,128]{1,0:T(8,128)(2,1)S(1)} %slice.215), channel_id=1, source_target_pairs={{0,2},{1,3},{2,0},{3,1},{4,6},{5,7},{6,4},{7,5},{8,10},{9,11},{10,... | collective-permute-start | bytes 307208 | tf_op jit(solution)/shard_map/ppermute | solution.py:592
  47.6 8.2 %collective-permute-start.20 = (bf16[4,800,128]{2,1,0:T(8,128)(2,1)S(1)}, bf16[4,800,128]{2,1,0:T(8,128)(2,1)}, u32[]{:S(2)}, u32[]{:S(2)}) collective-permute-start(bf16[4,800,128]{2,1,0:T(8,128)(2,1)S(1)} %pad_maximum_fusion.1.refs_1_), channel_id=1, source_target_pairs={{0,1},{1,0},{2,3},{3,2},{4,5},{5,4},{6,7},{7,6},{8,9},{9,8},{10,11... | collective-permute-start | bytes 2457608 | tf_op jit(solution)/shard_map/ppermute | solution.py:592
  82.1 8.4 %collective-permute-start.29 = (f32[8,1536]{1,0:T(8,128)S(1)}, f32[8,1536]{1,0:T(8,128)S(1)}, u32[]{:S(2)}, u32[]{:S(2)}) collective-permute-start(f32[8,1536]{1,0:T(8,128)S(1)} %add_add_fusion.7), channel_id=1, source_target_pairs={{0,24},{1,25},{2,26},{3,27},{4,28},{5,29},{6,30},{7,31},{8,16},{9,... | collective-permute-start | bytes 147464 | tf_op jit(solution)/shard_map/ppermute | solution.py:592
  206.2 15.9 %collective-permute-start.50 = (f32[8,1536]{1,0:T(8,128)S(1)}, f32[8,1536]{1,0:T(8,128)S(1)}, u32[]{:S(2)}, u32[]{:S(2)}) collective-permute-start(f32[8,1536]{1,0:T(8,128)S(1)} %add_add_fusion.1), channel_id=1, source_target_pairs={{0,24},{1,25},{2,26},{3,27},{4,28},{5,29},{6,30},{7,31},{8,16},{9,... | collective-permute-start | bytes 147464 | tf_op jit(solution)/shard_map/ppermute | solution.py:592
  208.3 13.8 %collective-permute-start.49 = (f32[8,1536]{1,0:T(8,128)S(1)}, f32[8,1536]{1,0:T(8,128)S(1)}, u32[]{:S(2)}, u32[]{:S(2)}) collective-permute-start(f32[8,1536]{1,0:T(8,128)S(1)} %add_add_fusion.1), channel_id=1, source_target_pairs={{0,16},{1,17},{2,18},{3,19},{4,20},{5,21},{6,22},{7,23},{8,24},{9,... | collective-permute-start | bytes 147464 | tf_op jit(solution)/shard_map/ppermute | solution.py:592
  208.8 13.4 %collective-permute-start.48 = (f32[8,1536]{1,0:T(8,128)S(1)}, f32[8,1536]{1,0:T(8,128)S(1)}, u32[]{:S(2)}, u32[]{:S(2)}) collective-permute-start(f32[8,1536]{1,0:T(8,128)S(1)} %add_add_fusion.1), channel_id=1, source_target_pairs={{0,8},{1,9},{2,10},{3,11},{4,12},{5,13},{6,14},{7,15},{8,0},{9,1},... | collective-permute-start | bytes 147464 | tf_op jit(solution)/shard_map/ppermute | solution.py:592
  251.0 20.6 %collective-permute-start.54 = (bf16[4,2,400,128]{3,2,1,0:T(8,128)(2,1)}, bf16[4,2,400,128]{3,2,1,0:T(8,128)(2,1)}, u32[]{:S(2)}, u32[]{:S(2)}) collective-permute-start(bf16[4,2,400,128]{3,2,1,0:T(8,128)(2,1)} %slice.220), channel_id=1, source_target_pairs={{0,4},{1,5},{2,6},{3,7},{4,0},{5,1},{6,2},{7,3},{8,12},{9,13},{10,... | collective-permute-start | bytes 2457608 | tf_op jit(solution)/shard_map/ppermute | solution.py:592
  251.4 22.1 %collective-permute-start.52 = (bf16[4,2,400,128]{3,2,0,1:T(8,128)(2,1)S(1)}, bf16[4,2,400,128]{3,2,0,1:T(8,128)(2,1)S(1)}, u32[]{:S(2)}, u32[]{:S(2)}) collective-permute-start(bf16[4,2,400,128]{3,2,0,1:T(8,128)(2,1)S(1)} %copy.49), channel_id=1, source_target_pairs={{0,2},{1,3},{2,0},{3,1},{4,6},{5,7},{6,4},{7,5},{8,10},{9,11},{10,... | collective-permute-start | bytes 2457608 | tf_op jit(solution)/shard_map/ppermute | solution.py:592
  272.9 10.7 %collective-permute-start.55 = (bf16[4,400,128]{2,1,0:T(8,128)(2,1)S(1)}, bf16[4,400,128]{2,1,0:T(8,128)(2,1)S(1)}, u32[]{:S(2)}, u32[]{:S(2)}) collective-permute-start(bf16[4,400,128]{2,1,0:T(8,128)(2,1)S(1)} %slice_bitcast_fusion), channel_id=1, source_target_pairs={{0,2},{1,3},{2,0},{3,1},{4,6},{5,7},{6,4},{7,5},{8,10},{9,11},{10,... | collective-permute-start | bytes 1228808 | tf_op jit(solution)/shard_map/ppermute | solution.py:592
  273.6 10.5 %collective-permute-start.53 = (bf16[4,400,128]{2,1,0:T(8,128)(2,1)S(1)}, bf16[4,400,128]{2,1,0:T(8,128)(2,1)S(1)}, u32[]{:S(2)}, u32[]{:S(2)}) collective-permute-start(bf16[4,400,128]{2,1,0:T(8,128)(2,1)S(1)} %slice_bitcast_fusion.2), channel_id=1, source_target_pairs={{0,4},{1,5},{2,6},{3,7},{4,0},{5,1},{6,2},{7,3},{8,12},{9,13},{10,... | collective-permute-start | bytes 1228808 | tf_op jit(solution)/shard_map/ppermute | solution.py:592
  284.2 10.0 %collective-permute-start.56 = (bf16[800,128]{1,0:T(8,128)(2,1)S(1)}, bf16[800,128]{1,0:T(8,128)(2,1)S(1)}, u32[]{:S(2)}, u32[]{:S(2)}) collective-permute-start(bf16[800,128]{1,0:T(8,128)(2,1)S(1)} %get-tuple-element.93), channel_id=1, source_target_pairs={{0,8},{1,9},{2,10},{3,11},{4,12},{5,13},{6,14},{7,15},{8,16},{9,17... | collective-permute-start | bytes 614408 | tf_op jit(solution)/shard_map/ppermute | solution.py:596
  284.4 9.8 %collective-permute-start.58 = (bf16[800,128]{1,0:T(8,128)(2,1)S(1)}, bf16[800,128]{1,0:T(8,128)(2,1)S(1)}, u32[]{:S(2)}, u32[]{:S(2)}) collective-permute-start(bf16[800,128]{1,0:T(8,128)(2,1)S(1)} %get-tuple-element.94), channel_id=1, source_target_pairs={{0,24},{1,25},{2,26},{3,27},{4,28},{5,29},{6,30},{7,31},{8,0},{9,1... | collective-permute-start | bytes 614408 | tf_op jit(solution)/shard_map/ppermute | solution.py:596
  288.1 15.0 %collective-permute-start.57 = (bf16[800,128]{1,0:T(8,128)(2,1)S(1)}, bf16[800,128]{1,0:T(8,128)(2,1)S(1)}, u32[]{:S(2)}, u32[]{:S(2)}) collective-permute-start(bf16[800,128]{1,0:T(8,128)(2,1)S(1)} %get-tuple-element.95), channel_id=1, source_target_pairs={{0,16},{1,17},{2,18},{3,19},{4,20},{5,21},{6,22},{7,23},{8,24},{9,... | collective-permute-start | bytes 614408 | tf_op jit(solution)/shard_map/ppermute | solution.py:596
  (54 other events, 476.1 us)
